TPU v7x, 32 devices: a whole 2x2x4 slice. The times are simulated.
32 devices in a mesh: band: 8 (over z, y), lon: 4 (over x, core).
Axes of the slice: x: 2, y: 2, z: 4, core: 2. Of those that a mesh axis runs over, the one named last changes fastest.
Arguments:
- node_state: bfloat16 [65536, 64], P(('band', 'lon')), may hold values from -6 to 6
- latent: bfloat16 [65536, 64], P(('band', 'lon')), may hold values from -6 to 6
- edge_attr: bfloat16 [2, 65536, 8, 64], P(None, ('band', 'lon')), may hold values from -6 to 6
- neighbours: int32 [2, 65536, 8], P(None, ('band', 'lon')), may hold values from 0 to 2559
- halo_lists: int32 [128, 128], P(('band', 'lon')), may hold values from 0 to 1023
- valid_counts: int32 [32], P(('band', 'lon')), may hold values from 1024 to 2048
- channel_mask: int32 [2, 64], replicated, may hold values 0 or 1
- edge_w1: bfloat16 [2, 192, 64], replicated, may hold values from -0.4375 to 0.4375
- edge_b1: float32 [2, 64], replicated, may hold values from -3 to 3
- edge_w2: bfloat16 [2, 64, 64], replicated, may hold values from -0.75 to 0.75
- edge_gain: float32 [2, 64], replicated, may hold values from 0.25 to 1.75
- edge_shift: float32 [2, 64], replicated, may hold values from -2 to 2
- node_w1: bfloat16 [2, 128, 64], replicated, may hold values from -0.5 to 0.5
- node_b1: float32 [2, 64], replicated, may hold values from -3 to 3
- node_w2: bfloat16 [2, 64, 64], replicated, may hold values from -0.75 to 0.75
- node_gain: float32 [2, 64], replicated, may hold values from 0.25 to 1.75
- node_shift: float32 [2, 64], replicated, may hold values from -2 to 2
- out_grad: bfloat16 [65536, 64], P(('band', 'lon')), may hold values from -6 to 6
Outputs:
- mesh_out: bfloat16 [65536, 64], P(('band', 'lon'))
- grad_state: float32 [65536, 64], P(('band', 'lon'))
- grad_latent: float32 [65536, 64], P(('band', 'lon'))
- grad_edge_w1: float32 [2, 192, 64], replicated
- grad_edge_b1: float32 [2, 64], replicated
- grad_edge_w2: float32 [2, 64, 64], replicated
- grad_edge_gain: float32 [2, 64], replicated
- grad_edge_shift: float32 [2, 64], replicated
- grad_node_w1: float32 [2, 128, 64], replicated
- grad_node_b1: float32 [2, 64], replicated
- grad_node_w2: float32 [2, 64, 64], replicated
- grad_node_gain: float32 [2, 64], replicated
- grad_node_shift: float32 [2, 64], replicated
Inputs may be any that keep to these rules, and one draw needn't show every extreme that they name: `neighbours`: values below 2048 name this device's own rows; the next four blocks of 128 name the rows from the band below, the band above, the sector west and the sector east, in order. `halo_lists`: rows of the device itself, always below its live count.
All inputs are finite; a program needn't handle non-finite values.
Results may differ from a plain program's by a relative error of at most 0.012.
Values may be sent and summed in bfloat16 or wider, within the bound.
A program may use at most 128 MiB of HBM per device.

v0:
```python
import functools
import types

import jax
import jax.numpy as jnp
from jax import lax
from jax.experimental import pallas as pl
from jax.experimental.pallas import tpu as pltpu
from jax.sharding import PartitionSpec as P

F32 = jnp.float32
BF16 = jnp.bfloat16
MESH = pl.DeviceIdType.MESH
LISTED = 1024
TILE_F, TILE_B, TILE_S = 2048, 2048, 1024
GROUP_F, GROUP_B, GROUP_S = 2, 2, 4
WAYS = 4
CHUNK = 256
EB1, EGAIN, ESHIFT, NB1, NGAIN, NSHIFT, CMASK = range(7)


def dot(left, right):
    return jnp.dot(left, right, preferred_element_type=F32)


def dot_nt(left, right):
    return lax.dot_general(left, right, (((1,), (1,)), ((), ())), preferred_element_type=F32)


def exact_dot(left, right, dims):
    return lax.dot_general(
        left, right, (dims, ((), ())), precision=lax.Precision.HIGHEST, preferred_element_type=F32
    )


def eye(size, kind):
    row = lax.broadcasted_iota(jnp.int32, (size, size), 0)
    col = lax.broadcasted_iota(jnp.int32, (size, size), 1)
    return (row == col).astype(F32).astype(kind)


def turned(matrix):
    return dot_nt(eye(matrix.shape[1], BF16), matrix).astype(BF16)


def one_hot(row, total):
    width = row.shape[1]
    index = lax.broadcasted_iota(jnp.int16, (total, width), 0)
    return jnp.where(
        index == jnp.broadcast_to(row.astype(jnp.int16), (total, width)), BF16(1), BF16(0)
    )


def join(parts):
    return parts[0] if len(parts) == 1 else jnp.concatenate(parts, axis=1)


def mean0(values):
    return jnp.mean(values, axis=0, keepdims=True)


def gate(half):
    bend = jnp.tanh(half)
    act = half + half * bend
    return act, (1.0 + bend) + act * (1.0 - bend)


def fold(values):
    total = values[:, :128]
    for at in range(128, values.shape[1], 128):
        total = total + values[:, at : at + 128]
    return total


def kernel(names, bands, lons, *refs):
    k = types.SimpleNamespace(**dict(zip(names, refs)))
    band, lon = lax.axis_index("band"), lax.axis_index("lon")
    wide, nodes = k.state.shape
    degree = k.nbr.shape[1]
    halo = k.lists.shape[1]
    high = WAYS * halo
    shift = high.bit_length() - 1
    locals_ = nodes // high
    parts = locals_ + 4 // WAYS
    count = k.count[0]
    fetch = {
        name: pltpu.make_async_copy(getattr(k, name + "_in"), getattr(k, name), k.load_sem.at[at])
        for at, name in enumerate(FETCHED)
    }
    for layer in range(2):
        fetch["attr", layer] = pltpu.make_async_copy(
            k.attr_in.at[layer], k.attr.at[layer], k.load_sem.at[len(FETCHED) + layer]
        )
    stores = [
        pltpu.make_async_copy(source, target, k.store_sem.at[at])
        for at, (source, target) in enumerate(
            (
                (k.mesh_out, k.mesh_to),
                (k.grad_latent, k.latent_to),
                (k.grad_state, k.state_to),
                (k.whole, k.reduced),
            )
        )
    ]
    west, east = lax.rem(lon + lons - 1, lons), lax.rem(lon + 1, lons)
    has_low, has_high = band > 0, band < bands - 1

    near = 2 if bands % 2 == 0 else 1
    size_a, size_b = near * lons, bands // near
    at_a = lax.rem(band, near) * lons + lon
    at_b = band // near

    def member_a(at):
        return (at_b * near + at // lons, lax.rem(at, lons))

    def member_b(at):
        return (at * near + lax.rem(band, near), lon)

    def over(size, here, act):
        def step(at, carry):
            act(lax.rem(here + at, size))
            return carry

        lax.fori_loop(1, size, step, 0)

    for use in range(2):
        for way in range(2):
            k.halos[use, way] = jnp.zeros((wide, halo), BF16)
            k.backs[use, way] = jnp.zeros((wide, halo), BF16)
    barrier = pltpu.get_barrier_semaphore()

    def greet(device):
        pl.semaphore_signal(barrier, inc=1, device_id=device, device_id_type=MESH)

    pl.when(has_low)(lambda: greet((band - 1, lon)))
    pl.when(has_high)(lambda: greet((band + 1, lon)))
    over(size_a, at_a, lambda at: greet(member_a(at)))
    over(size_b, at_b, lambda at: greet(member_b(at)))
    greeted = size_a + size_b - 2 + has_low.astype(jnp.int32) + has_high.astype(jnp.int32)
    for name in FETCHED[:2]:
        fetch[name].start()
    fetch["attr", 0].start()
    for name in FETCHED[2:]:
        fetch[name].start()
    fetch["attr", 1].start()

    def exchange(source, target, sends, recvs, use):
        def copy(block, landing, device):
            return pltpu.make_async_remote_copy(
                src_ref=source.at[use, block],
                dst_ref=target.at[use, landing],
                send_sem=sends.at[use, block],
                recv_sem=recvs.at[use, landing],
                device_id=device,
                device_id_type=MESH,
            )

        return copy

    turn = (1, 0, 3, 2)

    def targets():
        return ((band - 1, lon), (band + 1, lon), (band, west), (band, east))

    def start_exchange(copy):
        peers = targets()
        for block in range(4):
            go = copy(block, turn[block], peers[block]).start
            if block == 0:
                pl.when(has_low)(go)
            elif block == 1:
                pl.when(has_high)(go)
            else:
                go()

    def finish_exchange(copy):
        peers = targets()
        for block in range(4):
            def end(block=block):
                copy(block, block, peers[block]).wait()

            if block == 0:
                pl.when(has_low)(end)
            elif block == 1:
                pl.when(has_high)(end)
            else:
                end()

    SENDER, RECEIVER, ATTR, SECOND, NODE_TWO, SENDER_B, RECEIVER_B, SECOND_B, NODE_TWO_B = range(9)

    def col(layer, which):
        at = 2 * which + layer
        return k.cols[:, at : at + 1]

    def tables():
        for at, rows in enumerate((k.eb1, k.egain, k.eshift, k.nb1, k.ngain, k.nshift)):
            k.vrows[2 * at : 2 * at + 2, :] = rows[...]
        k.vrows[12:14, :] = k.cmask[...].astype(F32)
        k.vrows[14:16, :] = jnp.zeros((2, wide), F32)
        k.cols[...] = exact_dot(eye(wide, F32), k.vrows[...], ((1,), (1,)))

        weights = []
        for layer in range(2):
            w1t = k.ew1t[layer]
            n1t = k.nw1t[layer]
            w2 = k.ew2[layer]
            n2 = k.nw2[layer]
            half = BF16(0.5)
            weights.append(
                dict(
                    sender=w1t[:, :wide] * half,
                    receiver=w1t[:, wide : 2 * wide] * half,
                    attr=w1t[:, 2 * wide :] * half,
                    second=turned(w2),
                    node_one=n1t * half,
                    node_two=turned(n2),
                    sender_back=turned(w1t[:, :wide]),
                    receiver_back=turned(w1t[:, wide : 2 * wide]),
                    second_back=w2 * half,
                    node_one_back=turned(n1t),
                    node_two_back=n2 * half,
                )
            )
        for layer in range(2):
            for at, name in enumerate(
                (
                    "sender", "receiver", "attr", "second", "node_two",
                    "sender_back", "receiver_back", "second_back", "node_two_back",
                )
            ):
                k.small[layer, at] = weights[layer][name]
            k.wide_w[layer] = weights[layer]["node_one"]
            k.tall_w[layer] = weights[layer]["node_one_back"]

    def owners():
        for way in range(4):
            k.owner[:, way * halo : (way + 1) * halo] = one_hot(k.lists[way : way + 1, :], LISTED)

    def split_index(layer, lanes):
        index = k.nbr[layer, :, lanes]
        return index, index >> shift, index & (high - 1)

    def live_lanes(start, width):
        return lax.broadcasted_iota(jnp.int32, (1, width), 1) + start < count

    def node_lanes(first, last):
        return [pl.ds(at, CHUNK) for at in range(first, last, CHUNK)]

    def pick_halos(layer):
        picked = dot(k.xs[layer, :wide, :LISTED], k.owner[...]).astype(BF16)
        for way in range(4):
            k.sends[layer, way] = picked[:, way * halo : (way + 1) * halo]

    def send_halos(layer):
        start_exchange(exchange(k.sends, k.halos, k.halo_send, k.halo_recv, layer))

    def as_sent(layer, rows):
        return rows if layer == 0 else dot(k.small[layer, SENDER], rows).astype(BF16)

    def project(layer):
        low = k.xs[layer, :wide, :]
        own = as_sent(layer, low)
        for part in range(locals_):
            k.table[part * wide : (part + 1) * wide, :] = own[:, part * high : (part + 1) * high]
        base = dot(k.small[layer, RECEIVER], low) + 0.5 * col(layer, EB1)
        fetch["attr", layer].wait()
        for j in range(degree):
            k.pre[j] = dot(k.small[layer, ATTR], k.attr[layer, j]) + base

    def project_halos(layer):
        finish_exchange(exchange(k.sends, k.halos, k.halo_send, k.halo_recv, layer))
        for way in range(4):
            top, left = (locals_ + way // WAYS) * wide, way % WAYS * halo
            k.table[top : top + wide, left : left + halo] = as_sent(layer, k.halos[layer, way])

    def edges_forward(layer):
        def body(at, carry):
            start = pl.multiple_of(at * TILE_F, TILE_F)
            lanes = pl.ds(start, TILE_F)
            index, sub, hi = split_index(layer, lanes)
            sender_ok = jnp.where(
                index < nodes,
                (index < count).astype(F32),
                jnp.where(
                    index < nodes + halo,
                    has_low.astype(F32),
                    jnp.where(index < nodes + 2 * halo, has_high.astype(F32), 1.0),
                ),
            )
            edge_ok = sender_ok * live_lanes(start, TILE_F).astype(F32)
            total = jnp.zeros((wide, TILE_F), F32)
            for first in range(0, degree, GROUP_F):
                slots = range(first, first + GROUP_F)
                hot = join([one_hot(hi[j : j + 1], high) for j in slots])
                found = dot(k.table[...], hot)
                for place, j in enumerate(slots):
                    piece = found[:, place * TILE_F : (place + 1) * TILE_F]
                    piece = piece.reshape(parts, wide // 8, 8, TILE_F)
                    which = jnp.broadcast_to(sub[j : j + 1], (8, TILE_F))
                    chosen = piece[0]
                    for part in range(1, parts):
                        chosen = jnp.where((which == part)[None], piece[part], chosen)
                    chosen = chosen.reshape(wide, TILE_F)
                    if layer == 0:
                        chosen = chosen.astype(BF16)
                        k.senders[j, :, lanes] = chosen
                        chosen = dot(k.small[layer, SENDER], chosen)
                    act, slope = gate(chosen + k.pre[j, :, lanes])
                    act = act.astype(BF16)
                    k.act[layer, j, :, lanes] = act
                    k.slope[layer, j, :, lanes] = slope.astype(BF16)
                    second = dot(k.small[layer, SECOND], act)
                    center = second - mean0(second)
                    rate = lax.rsqrt(mean0(center * center) + 1e-05) * edge_ok[j : j + 1]
                    k.rate_e[layer, j : j + 1, lanes] = rate
                    unit = center * rate
                    k.unit[layer, j, :, lanes] = unit.astype(BF16)
                    total = total + unit
            k.total[layer, :, lanes] = total
            k.kept[layer, :, lanes] = jnp.sum(edge_ok, axis=0, keepdims=True)
            return carry

        lax.fori_loop(0, nodes // TILE_F, body, 0)

    def nodes_forward(layer, first, last):
        for lanes in node_lanes(first, last):
            mask = col(layer, CMASK)
            summed = (mask * col(layer, EGAIN)) * k.total[layer, :, lanes] + (
                mask * col(layer, ESHIFT)
            ) * k.kept[layer, :, lanes]
            k.xs[layer, wide:, lanes] = summed.astype(BF16)
            half = dot(k.wide_w[layer], k.xs[layer, :, lanes]) + 0.5 * col(layer, NB1)
            act, slope = gate(half)
            act = act.astype(BF16)
            k.act_n[layer, :, lanes] = act
            k.slope_n[layer, :, lanes] = slope.astype(BF16)
            fourth = dot(k.small[layer, NODE_TWO], act)
            center = fourth - mean0(fourth)
            rate = lax.rsqrt(mean0(center * center) + 1e-05)
            unit = center * rate
            k.rate_n[layer, :, lanes] = rate
            k.unit_n[layer, :, lanes] = unit
            valid = live_lanes(lanes.start, CHUNK).astype(F32)
            change = valid * (unit * col(layer, NGAIN) + col(layer, NSHIFT))
            if layer == 0:
                middle = k.state[:, lanes].astype(F32) + change + k.latent[:, lanes].astype(F32)
                k.middle[:, lanes] = middle
                k.xs[1, :wide, lanes] = middle.astype(BF16)
            else:
                k.mesh_out[:, lanes] = (k.middle[:, lanes] + change).astype(BF16)

    def into(layer):
        return k.grad_latent if layer == 1 else k.grad_state

    def nodes_backward(layer, first, last):
        for lanes in node_lanes(first, last):
            valid = live_lanes(lanes.start, CHUNK).astype(F32)
            if layer == 1:
                grad = k.out_grad[:, lanes].astype(F32)
            else:
                grad = k.grad_latent[:, lanes]
            unit = k.unit_n[layer, :, lanes]
            grad_ok = valid * grad
            k.sums[layer, NGAIN] += fold(grad_ok * unit)
            k.sums[layer, NSHIFT] += fold(grad_ok)
            scaled = grad_ok * col(layer, NGAIN)
            fourth = k.rate_n[layer, :, lanes] * (
                scaled - mean0(scaled) - unit * mean0(scaled * unit)
            )
            fourth = fourth.astype(BF16)
            k.acc_64[layer, 3] += dot_nt(k.act_n[layer, :, lanes], fourth)
            third = dot(k.small[layer, NODE_TWO_B], fourth) * k.slope_n[layer, :, lanes].astype(F32)
            k.sums[layer, NB1] += fold(third)
            third = third.astype(BF16)
            k.acc_128[layer] += dot_nt(third, k.xs[layer, :, lanes])
            both = dot(k.tall_w[layer], third)
            into(layer)[:, lanes] = grad + both[:wide]
            masked = both[wide:] * col(layer, CMASK)
            k.sums[layer, EGAIN] += fold(masked * k.total[layer, :, lanes])
            k.sums[layer, ESHIFT] += fold(masked * k.kept[layer, :, lanes])
            scaled = masked * col(layer, EGAIN)
            k.scaled[:, lanes] = scaled
            k.center[:, lanes] = scaled - mean0(scaled)

    def scatter_slots(lanes, sub, hi, firsts, slots):
        spreads, hots = [], []
        for j, grad in zip(slots, firsts):
            width = grad.shape[1]
            which = jnp.broadcast_to(sub[j : j + 1].astype(jnp.int16), (16, width))
            rows = grad.reshape(wide // 16, 16, width)
            spreads.append(
                jnp.concatenate(
                    [
                        jnp.where((which == part)[None], rows, BF16(0)).reshape(wide, width)
                        for part in range(parts)
                    ],
                    axis=0,
                )
            )
            hots.append(one_hot(hi[j : j + 1], high))
        k.scatter[...] += dot_nt(join(spreads), join(hots))

    def scatter_pass(layer, between):
        def body(at, carry):
            lanes = pl.ds(pl.multiple_of(at * TILE_S, TILE_S), TILE_S)
            index, sub, hi = split_index(layer, lanes)
            for start in range(0, degree, GROUP_S):
                slots = range(start, start + GROUP_S)
                scatter_slots(lanes, sub, hi, [k.first[j, :, lanes] for j in slots], slots)
            pl.when(at == 0)(between)
            return carry

        lax.fori_loop(0, nodes // TILE_S, body, 0)

    def edges_backward(layer):
        def body(at, carry):
            lanes = pl.ds(pl.multiple_of(at * TILE_B, TILE_B), TILE_B)
            index, sub, hi = split_index(layer, lanes)
            scaled, center = k.scaled[:, lanes], k.center[:, lanes]
            first_sum = jnp.zeros((wide, TILE_B), F32)
            for start in range(0, degree, GROUP_B):
                slots = range(start, start + GROUP_B)
                firsts = []
                for j in slots:
                    unit = k.unit[layer, j, :, lanes].astype(F32)
                    second = (center - unit * mean0(scaled * unit)) * k.rate_e[
                        layer, j : j + 1, lanes
                    ]
                    second = second.astype(BF16)
                    grad_one = dot(k.small[layer, SECOND_B], second) * k.slope[
                        layer, j, :, lanes
                    ].astype(F32)
                    first_sum = first_sum + grad_one
                    grad_one = grad_one.astype(BF16)
                    k.first[j, :, lanes] = grad_one
                    k.second[j, :, lanes] = second
                    firsts.append(grad_one)
                if layer == 1:
                    scatter_slots(lanes, sub, hi, firsts, slots)
            k.first_sum[:, lanes] = first_sum
            return carry

        lax.fori_loop(0, nodes // TILE_B, body, 0)

    def edge_weights(layer):
        grad_two = jnp.zeros((wide, wide), F32)
        grad_attr = jnp.zeros((wide, wide), F32)
        grad_both = jnp.zeros((wide, 2 * wide), F32)
        for j in range(degree):
            grad_two = grad_two + dot_nt(k.act[layer, j], k.second[j])
            if layer == 0:
                both = jnp.concatenate([k.senders[j], k.attr[layer, j]], axis=0)
                grad_both = grad_both + dot_nt(k.first[j], both)
            else:
                grad_attr = grad_attr + dot_nt(k.first[j], k.attr[layer, j])
        k.acc_64[layer, 2] = grad_two
        if layer == 0:
            k.acc_64[layer, 0] = grad_both[:, :wide]
            k.acc_64[layer, 1] = grad_both[:, wide:]
        else:
            k.acc_64[layer, 1] = grad_attr

    def two_terms(values):
        coarse = values.astype(BF16)
        return coarse, (values - coarse.astype(F32)).astype(BF16)

    def give_back(layer):
        back = k.small[layer, SENDER_B]
        halo_sums = [
            two_terms(k.scatter[part * wide : (part + 1) * wide, :])
            for part in range(locals_, parts)
        ]
        to_owner = join([dot(back, coarse) + dot(back, fine) for coarse, fine in halo_sums])
        to_owner = to_owner.astype(BF16)
        for way in range(4):
            k.gives[layer, way] = to_owner[:, way * halo : (way + 1) * halo]
        start_exchange(exchange(k.gives, k.backs, k.back_send, k.back_recv, layer))

    def sender_weights(layer):
        sender = jnp.zeros((wide, wide), F32)
        for part in range(parts):
            if part < locals_:
                rows = k.xs[layer, :wide, part * high : (part + 1) * high]
            else:
                first = (part - locals_) * WAYS
                rows = join([k.halos[layer, first + way] for way in range(WAYS)])
            coarse, fine = two_terms(k.scatter[part * wide : (part + 1) * wide, :])
            sender = sender + dot_nt(coarse, rows) + dot_nt(fine, rows)
        k.acc_64[layer, 0] = sender

    def share_weights(layer):
        k.sums[layer, EB1] = fold(k.first_sum[...])
        first_sum = k.first_sum[...].astype(BF16)
        receiver = dot_nt(first_sum, k.xs[layer, :wide, :])
        sender = k.acc_64[layer, 0]
        lines = exact_dot(
            jnp.ones((8, 128), F32), k.sums[layer].reshape(6 * wide, 128), ((1,), (1,))
        )
        row = lax.broadcasted_iota(jnp.int32, (8, wide), 0)
        vectors = jnp.zeros((8, wide), F32)
        for which in range(6):
            vectors = jnp.where(
                row == which, lines[:, which * wide : (which + 1) * wide], vectors
            )
        vectors = jnp.concatenate([vectors, jnp.zeros((wide - 8, wide), F32)], axis=0)
        blocks = (
            join([sender, receiver]),
            join([k.acc_64[layer, 1], k.acc_64[layer, 2]]),
            k.acc_128[layer],
            join([k.acc_64[layer, 3], vectors]),
        )
        rows = k.share.shape[2]
        for at, block in enumerate(blocks):
            for piece in range(wide // rows):
                k.share[layer, at * (wide // rows) + piece] = block[
                    piece * rows : (piece + 1) * rows, :
                ].astype(WIRE)

    def own_rows(layer):
        back = k.small[layer, SENDER_B]
        first_sum = k.first_sum[...].astype(BF16)
        for part in range(locals_):
            place = slice(part * high, (part + 1) * high)
            coarse, fine = two_terms(k.scatter[part * wide : (part + 1) * wide, :])
            into(layer)[:, place] += (
                dot(back, coarse)
                + dot(back, fine)
                + dot(k.small[layer, RECEIVER_B], first_sum[:, place])
            )

    def take_back(layer):
        finish_exchange(exchange(k.gives, k.backs, k.back_send, k.back_recv, layer))
        returned = join([k.backs[layer, way] for way in range(4)])
        into(layer)[:, :LISTED] += dot_nt(returned, k.owner[...])

    def spread_copy(layer, slot, other):
        return pltpu.make_async_remote_copy(
            src_ref=k.share.at[layer, other],
            dst_ref=k.spread.at[layer, slot],
            send_sem=k.rs_send.at[layer, other],
            recv_sem=k.rs_recv.at[layer, slot],
            device_id=member_a(other),
            device_id_type=MESH,
        )

    def swap_copy(layer, slot, other):
        return pltpu.make_async_remote_copy(
            src_ref=k.swap.at[layer, at_b],
            dst_ref=k.swap.at[layer, slot],
            send_sem=k.sw_send.at[layer, other],
            recv_sem=k.sw_recv.at[layer, slot],
            device_id=member_b(other),
            device_id_type=MESH,
        )

    def gather_copy(layer, slot, other):
        return pltpu.make_async_remote_copy(
            src_ref=k.whole.at[layer, at_a],
            dst_ref=k.whole.at[layer, slot],
            send_sem=k.ag_send.at[layer, other],
            recv_sem=k.ag_recv.at[layer, slot],
            device_id=member_a(other),
            device_id_type=MESH,
        )

    def added(blocks):
        return jnp.sum(blocks.astype(F32), axis=0).astype(WIRE)

    def spread_start(layer):
        over(size_a, at_a, lambda other: spread_copy(layer, at_a, other).start())
        k.spread[layer, at_a] = k.share[layer, at_a]

    def swap_start(layer):
        over(size_a, at_a, lambda other: spread_copy(layer, other, other).wait())
        k.swap[layer, at_b] = added(k.spread[layer])
        over(size_b, at_b, lambda other: swap_copy(layer, at_b, other).start())

    def gather_start(layer):
        over(size_b, at_b, lambda other: swap_copy(layer, other, other).wait())
        k.whole[layer, at_a] = added(k.swap[layer])
        over(size_a, at_a, lambda other: gather_copy(layer, at_a, other).start())

    def gather_end(layer):
        over(size_a, at_a, lambda other: gather_copy(layer, other, other).wait())

    fetch["lists"].wait()
    owners()
    fetch["state"].wait()
    k.xs[0, :wide, :] = k.state[...]
    pick_halos(0)
    for name in FETCHED[2:-2]:
        fetch[name].wait()
    tables()
    pl.semaphore_wait(barrier, greeted)
    send_halos(0)
    k.sums[...] = jnp.zeros_like(k.sums)
    k.acc_64[...] = jnp.zeros_like(k.acc_64)
    k.acc_128[...] = jnp.zeros_like(k.acc_128)
    k.scatter[...] = jnp.zeros_like(k.scatter)
    project(0)
    project_halos(0)
    edges_forward(0)
    fetch["latent"].wait()
    nodes_forward(0, 0, LISTED)
    pick_halos(1)
    send_halos(1)
    nodes_forward(0, LISTED, nodes)
    project(1)
    project_halos(1)
    edges_forward(1)
    fetch["out_grad"].wait()
    nodes_forward(1, 0, nodes)
    stores[0].start()
    nodes_backward(1, 0, nodes)
    edges_backward(1)
    give_back(1)
    edge_weights(1)
    sender_weights(1)
    share_weights(1)
    spread_start(1)
    own_rows(1)
    nodes_backward(0, LISTED, nodes)
    take_back(1)
    stores[1].start()
    nodes_backward(0, 0, LISTED)
    edges_backward(0)
    edge_weights(0)
    share_weights(0)
    spread_start(0)
    swap_start(1)
    k.scatter[...] = jnp.zeros_like(k.scatter)
    scatter_pass(0, lambda: swap_start(0))
    give_back(0)
    gather_start(0)
    gather_start(1)
    own_rows(0)
    take_back(0)
    stores[2].start()
    gather_end(1)
    gather_end(0)
    stores[3].start()
    for store in stores:
        store.wait()


def finish(names, *refs):
    k = types.SimpleNamespace(**dict(zip(names, refs)))
    wide = k.g_ew2.shape[1]
    k.mesh_out[...] = k.mesh_in[...]
    k.grad_state[...] = k.state_in[...]
    k.grad_latent[...] = k.latent_in[...]
    for layer in range(2):
        rows = k.reduced.shape[2]
        pieces = wide // rows
        blocks = []
        for at in range(4):
            block = [k.reduced[layer, at * pieces + piece].astype(F32) for piece in range(pieces)]
            blocks.append(block[0] if pieces == 1 else jnp.concatenate(block, axis=0))
        k.g_ew1t[layer, :, : 2 * wide] = blocks[0]
        k.g_ew1t[layer, :, 2 * wide :] = blocks[1][:, :wide]
        k.g_ew2[layer] = blocks[1][:, wide:]
        k.g_nw1t[layer] = blocks[2]
        k.g_nw2[layer] = blocks[3][:, :wide]
        for which, out in enumerate(
            (k.g_eb1, k.g_egain, k.g_eshift, k.g_nb1, k.g_ngain, k.g_nshift)
        ):
            out[layer : layer + 1, :] = blocks[3][which : which + 1, wide:]


FETCHED = (
    "lists", "state", "nbr", "cmask", "ew1t", "eb1", "ew2", "egain", "eshift", "nw1t", "nb1",
    "nw2", "ngain", "nshift", "latent", "out_grad",
)
INPUTS = tuple(
    name if name == "count" else name + "_in"
    for name in (
        "state", "latent", "attr", "nbr", "lists", "count", "cmask", "ew1t", "eb1", "ew2",
        "egain", "eshift", "nw1t", "nb1", "nw2", "ngain", "nshift", "out_grad",
    )
)
OUTPUTS = (
    "mesh_out", "grad_state", "grad_latent", "g_ew1t", "g_eb1", "g_ew2", "g_egain",
    "g_eshift", "g_nw1t", "g_nb1", "g_nw2", "g_ngain", "g_nshift",
)


FIRST_OUTPUTS = ("mesh_to", "state_to", "latent_to", "reduced")
FINISH_INPUTS = ("mesh_in", "state_in", "latent_in", "reduced")
VMEM_BYTES = 60 * 2**20
WIRE = F32


def shards(bands, lons, *args):
    (
        node_state, latent, edge_attr, neighbours, halo_lists, valid_counts, channel_mask,
        edge_w1, edge_b1, edge_w2, edge_gain, edge_shift,
        node_w1, node_b1, node_w2, node_gain, node_shift, out_grad,
    ) = args
    nodes, wide = node_state.shape
    degree = neighbours.shape[2]
    halo = halo_lists.shape[1]
    high = WAYS * halo
    parts = nodes // high + 4 // WAYS
    size_a = lons * (2 if bands % 2 == 0 else 1)
    size_b = bands * lons // size_a
    rows = 4 * wide // size_a
    arrays = (
        node_state.T,
        latent.T,
        edge_attr.transpose(0, 2, 3, 1),
        neighbours.transpose(0, 2, 1),
        halo_lists,
        valid_counts,
        channel_mask,
        edge_w1.transpose(0, 2, 1),
        edge_b1,
        edge_w2,
        edge_gain,
        edge_shift,
        node_w1.transpose(0, 2, 1),
        node_b1,
        node_w2,
        node_gain,
        node_shift,
        out_grad.T,
    )
    shape = jax.ShapeDtypeStruct
    outs = (
        shape((wide, nodes), BF16),
        shape((wide, nodes), F32),
        shape((wide, nodes), F32),
        shape((2, wide, 3 * wide), F32),
        shape((2, wide), F32),
        shape((2, wide, wide), F32),
        shape((2, wide), F32),
        shape((2, wide), F32),
        shape((2, wide, 2 * wide), F32),
        shape((2, wide), F32),
        shape((2, wide, wide), F32),
        shape((2, wide), F32),
        shape((2, wide), F32),
    )
    sem = pltpu.SemaphoreType.DMA
    scratch = dict(
        halos=pltpu.VMEM((2, 4, wide, halo), BF16),
        backs=pltpu.VMEM((2, 4, wide, halo), BF16),
        sends=pltpu.VMEM((2, 4, wide, halo), BF16),
        gives=pltpu.VMEM((2, 4, wide, halo), BF16),
        share=pltpu.VMEM((2, size_a, rows, 128), WIRE),
        spread=pltpu.VMEM((2, size_a, rows, 128), WIRE),
        swap=pltpu.VMEM((2, size_b, rows, 128), WIRE),
        whole=pltpu.VMEM((2, size_a, rows, 128), WIRE),
        vrows=pltpu.VMEM((16, wide), F32),
        cols=pltpu.VMEM((wide, 16), F32),
        owner=pltpu.VMEM((LISTED, 4 * halo), BF16),
        small=pltpu.VMEM((2, 9, wide, wide), BF16),
        wide_w=pltpu.VMEM((2, wide, 2 * wide), BF16),
        tall_w=pltpu.VMEM((2, 2 * wide, wide), BF16),
        xs=pltpu.VMEM((2, 2 * wide, nodes), BF16),
        attr=pltpu.VMEM((2, degree, wide, nodes), BF16),
        mesh_out=pltpu.VMEM((wide, nodes), BF16),
        grad_latent=pltpu.VMEM((wide, nodes), F32),
        grad_state=pltpu.VMEM((wide, nodes), F32),
        load_sem=sem((len(FETCHED) + 2,)),
        store_sem=sem((4,)),
        pre=pltpu.VMEM((degree, wide, nodes), F32),
        senders=pltpu.VMEM((degree, wide, nodes), BF16),
        first=pltpu.VMEM((degree, wide, nodes), BF16),
        second=pltpu.VMEM((degree, wide, nodes), BF16),
        table=pltpu.VMEM((parts * wide, high), BF16),
        act=pltpu.VMEM((2, degree, wide, nodes), BF16),
        slope=pltpu.VMEM((2, degree, wide, nodes), BF16),
        unit=pltpu.VMEM((2, degree, wide, nodes), BF16),
        rate_e=pltpu.VMEM((2, degree, nodes), F32),
        total=pltpu.VMEM((2, wide, nodes), F32),
        kept=pltpu.VMEM((2, 1, nodes), F32),
        act_n=pltpu.VMEM((2, wide, nodes), BF16),
        slope_n=pltpu.VMEM((2, wide, nodes), BF16),
        rate_n=pltpu.VMEM((2, 1, nodes), F32),
        unit_n=pltpu.VMEM((2, wide, nodes), F32),
        middle=pltpu.VMEM((wide, nodes), F32),
        scaled=pltpu.VMEM((wide, nodes), F32),
        center=pltpu.VMEM((wide, nodes), F32),
        first_sum=pltpu.VMEM((wide, nodes), F32),
        scatter=pltpu.VMEM((parts * wide, high), F32),
        sums=pltpu.VMEM((2, 6, wide, 128), F32),
        acc_64=pltpu.VMEM((2, 4, wide, wide), F32),
        acc_128=pltpu.VMEM((2, wide, 2 * wide), F32),
        halo_send=sem((2, 4)),
        halo_recv=sem((2, 4)),
        back_send=sem((2, 4)),
        back_recv=sem((2, 4)),
        rs_send=sem((2, size_a)),
        rs_recv=sem((2, size_a)),
        sw_send=sem((2, size_b)),
        sw_recv=sem((2, size_b)),
        ag_send=sem((2, size_a)),
        ag_recv=sem((2, size_a)),
    )
    fetched = dict(zip(INPUTS, arrays))
    for name in FETCHED:
        array = fetched[name + "_in"]
        scratch[name] = pltpu.VMEM(array.shape, array.dtype)
    vmem = pl.BlockSpec(memory_space=pltpu.VMEM)
    anywhere = pl.BlockSpec(memory_space=pl.ANY)
    specs = [anywhere] * len(INPUTS)
    specs[INPUTS.index("count")] = pl.BlockSpec(memory_space=pltpu.SMEM)
    first_outs = outs[:3] + (shape((2, size_a, rows, 128), WIRE),)
    mids = pl.pallas_call(
        functools.partial(kernel, INPUTS + FIRST_OUTPUTS + tuple(scratch), bands, lons),
        out_shape=first_outs,
        in_specs=specs,
        out_specs=(anywhere,) * 4,
        scratch_shapes=list(scratch.values()),
        compiler_params=pltpu.CompilerParams(
            collective_id=0, has_side_effects=True, vmem_limit_bytes=VMEM_BYTES
        ),
        name="layers",
    )(*arrays)
    result = pl.pallas_call(
        functools.partial(finish, FINISH_INPUTS + OUTPUTS),
        out_shape=outs,
        in_specs=(vmem,) * 4,
        out_specs=(vmem,) * 13,
        compiler_params=pltpu.CompilerParams(vmem_limit_bytes=VMEM_BYTES),
        name="finish",
    )(*mids)
    result = list(result)
    for at in range(3):
        result[at] = result[at].T
    for at in (3, 8):
        result[at] = result[at].transpose(0, 2, 1)
    return tuple(result)


def solution(mesh):
    nodes = P(("band", "lon"), None)
    whole = P()
    in_specs = (
        nodes,
        nodes,
        P(None, ("band", "lon"), None, None),
        P(None, ("band", "lon"), None),
        nodes,
        P(("band", "lon")),
    ) + (whole,) * 11 + (nodes,)
    return jax.shard_map(
        functools.partial(shards, mesh.shape["band"], mesh.shape["lon"]),
        mesh=mesh,
        in_specs=in_specs,
        out_specs=(nodes,) * 3 + (whole,) * 10,
        check_vma=False,
    )
```

profile of v0, /device:TPU:0, one launch (start us, length us, event | category | flops | bytes accessed | tf_op | source)
XLA Modules:
  0.0 64.7 jit_solution(4807345925658944319)
XLA Ops:
  1.3 60.7 %layers.1 = (bf16[64,2048]{1,0:T(8,128)(2,1)}, f32[64,2048]{1,0:T(8,128)}, f32[64,2048]{1,0:T(8,128)}, f32[2,8,32,128]{3,2,1,0:T(8,128)}) custom-call(bf16[64,2048]{1,0:T(8,128)(2,1)} %bitcast.13, bf16[64,2048]{1,0:T(8,128)(2,1)} %bitcast.14, bf16[2,8,64,2048]{3,2,1,0:T(8,128)(2,1)} %bitcast.12, s32[2,8,2048]{2,1,0:T(8,128)} %bitcast.16, s32[4,128]{1,0:T(4,128)} %refs_4_.1, ...), custom_call_target="tpu_custom_call" | custom-call | tf_op jit(solution)/shard_map/layers/pallas_call | solution.py:809
  62.0 2.6 %finish.1 = (bf16[64,2048]{1,0:T(8,128)(2,1)}, f32[64,2048]{1,0:T(8,128)}, f32[64,2048]{1,0:T(8,128)}, f32[2,64,192]{2,1,0:T(8,128)}, f32[2,64]{1,0:T(2,128)}, /...) custom-call(bf16[64,2048]{1,0:T(8,128)(2,1)} %get-tuple-element.30.r, ...), custom_call_target="tpu_custom_call" | custom-call | tf_op jit(solution)/shard_map/finish/pallas_call | solution.py:820
where the time goes:
time: 64.9 us; the launch traced here: 64.7 us
  Pallas kernels  63.2 us (97%)
  between operations  1.43 us (2%)
    pallas_call x1, Pallas kernels, shards(): pl.pallas_call(functools.partial(kernel, INPUTS + FIRST_OUTPUTS + tuple(s...  60.7 us
    pallas_call x1, Pallas kernels, shards(): pl.pallas_call(functools.partial(finish, FINISH_INPUTS + OUTPUTS), out_sh...  2.56 us

commit v1 on v0

--- a/solution.py
+++ b/solution.py
@@ -12,8 +12,10 @@
 BF16 = jnp.bfloat16
 MESH = pl.DeviceIdType.MESH
 LISTED = 1024
-TILE_F, TILE_B, TILE_S = 2048, 2048, 1024
+TILE_B, TILE_S = 2048, 1024
 GROUP_F, GROUP_B, GROUP_S = 2, 2, 4
+LOOP_P, LOOP_W = 2, 2
+EARLY = 2
 WAYS = 4
 CHUNK = 256
 EB1, EGAIN, ESHIFT, NB1, NGAIN, NSHIFT, CMASK = range(7)
@@ -243,8 +245,9 @@
     def live_lanes(start, width):
         return lax.broadcasted_iota(jnp.int32, (1, width), 1) + start < count
 
-    def node_lanes(first, last):
-        return [pl.ds(at, CHUNK) for at in range(first, last, CHUNK)]
+    def over_nodes(first, last, act):
+        for start in range(first, last, CHUNK):
+            act(pl.ds(start, CHUNK))
 
     def pick_halos(layer):
         picked = dot(k.xs[layer, :wide, :LISTED], k.owner[...]).astype(BF16)
@@ -264,66 +267,95 @@
             k.table[part * wide : (part + 1) * wide, :] = own[:, part * high : (part + 1) * high]
         base = dot(k.small[layer, RECEIVER], low) + 0.5 * col(layer, EB1)
         fetch["attr", layer].wait()
-        for j in range(degree):
-            k.pre[j] = dot(k.small[layer, ATTR], k.attr[layer, j]) + base
+        k.base[...] = base
+
+        def attributes(at, carry):
+            for inner in range(degree // LOOP_P):
+                j = at * (degree // LOOP_P) + inner
+                k.pre[j] = dot(k.small[layer, ATTR], k.attr[layer, j]) + k.base[...]
+            return carry
+
+        lax.fori_loop(0, LOOP_P, attributes, 0)
 
     def project_halos(layer):
         finish_exchange(exchange(k.sends, k.halos, k.halo_send, k.halo_recv, layer))
-        for way in range(4):
-            top, left = (locals_ + way // WAYS) * wide, way % WAYS * halo
-            k.table[top : top + wide, left : left + halo] = as_sent(layer, k.halos[layer, way])
+        rows = join([k.halos[layer, way] for way in range(4)])
+        k.far[...] = rows.astype(F32) if layer == 0 else dot(k.small[layer, SENDER], rows)
+
+    def own_senders(layer, first):
+        slots = range(first, first + GROUP_F)
+        index, sub, hi = split_index(layer, slice(None))
+        found = dot(k.table[...], join([one_hot(hi[j : j + 1], high) for j in slots]))
+        rows = []
+        for place, j in enumerate(slots):
+            piece = found[:, place * nodes : (place + 1) * nodes]
+            piece = piece.reshape(locals_, wide // 8, 8, nodes)
+            which = jnp.broadcast_to(sub[j : j + 1], (8, nodes))
+            chosen = piece[0]
+            for part in range(1, locals_):
+                chosen = jnp.where((which == part)[None], piece[part], chosen)
+            rows.append(chosen.reshape(wide, nodes))
+        return rows
+
+    def with_halos(layer, j, own):
+        blocks = []
+        for start in range(0, nodes, 128):
+            index = jnp.broadcast_to(k.nbr[layer, j : j + 1, start : start + 128], (8, 128))
+            lane, way = index & (halo - 1), (index - nodes) >> (halo.bit_length() - 1)
+            rows = []
+            for top in range(0, wide, 8):
+                picked = own[top : top + 8, start : start + 128]
+                for at in range(4):
+                    block = k.far[top : top + 8, at * halo : (at + 1) * halo]
+                    block = jnp.take_along_axis(block, lane, axis=1, mode="promise_in_bounds")
+                    picked = jnp.where(way == at, block, picked)
+                rows.append(picked)
+            blocks.append(jnp.concatenate(rows, axis=0))
+        return join(blocks)
+
+    def edges_early(layer):
+        for first in range(0, EARLY, GROUP_F):
+            for place, rows in enumerate(own_senders(layer, first)):
+                k.early[first + place] = rows
 
     def edges_forward(layer):
-        def body(at, carry):
-            start = pl.multiple_of(at * TILE_F, TILE_F)
-            lanes = pl.ds(start, TILE_F)
-            index, sub, hi = split_index(layer, lanes)
-            sender_ok = jnp.where(
-                index < nodes,
-                (index < count).astype(F32),
-                jnp.where(
-                    index < nodes + halo,
-                    has_low.astype(F32),
-                    jnp.where(index < nodes + 2 * halo, has_high.astype(F32), 1.0),
-                ),
-            )
-            edge_ok = sender_ok * live_lanes(start, TILE_F).astype(F32)
-            total = jnp.zeros((wide, TILE_F), F32)
-            for first in range(0, degree, GROUP_F):
-                slots = range(first, first + GROUP_F)
-                hot = join([one_hot(hi[j : j + 1], high) for j in slots])
-                found = dot(k.table[...], hot)
-                for place, j in enumerate(slots):
-                    piece = found[:, place * TILE_F : (place + 1) * TILE_F]
-                    piece = piece.reshape(parts, wide // 8, 8, TILE_F)
-                    which = jnp.broadcast_to(sub[j : j + 1], (8, TILE_F))
-                    chosen = piece[0]
-                    for part in range(1, parts):
-                        chosen = jnp.where((which == part)[None], piece[part], chosen)
-                    chosen = chosen.reshape(wide, TILE_F)
-                    if layer == 0:
-                        chosen = chosen.astype(BF16)
-                        k.senders[j, :, lanes] = chosen
-                        chosen = dot(k.small[layer, SENDER], chosen)
-                    act, slope = gate(chosen + k.pre[j, :, lanes])
-                    act = act.astype(BF16)
-                    k.act[layer, j, :, lanes] = act
-                    k.slope[layer, j, :, lanes] = slope.astype(BF16)
-                    second = dot(k.small[layer, SECOND], act)
-                    center = second - mean0(second)
-                    rate = lax.rsqrt(mean0(center * center) + 1e-05) * edge_ok[j : j + 1]
-                    k.rate_e[layer, j : j + 1, lanes] = rate
-                    unit = center * rate
-                    k.unit[layer, j, :, lanes] = unit.astype(BF16)
-                    total = total + unit
-            k.total[layer, :, lanes] = total
-            k.kept[layer, :, lanes] = jnp.sum(edge_ok, axis=0, keepdims=True)
-            return carry
-
-        lax.fori_loop(0, nodes // TILE_F, body, 0)
+        index = k.nbr[layer]
+        sender_ok = jnp.where(
+            index < nodes,
+            (index < count).astype(F32),
+            jnp.where(
+                index < nodes + halo,
+                has_low.astype(F32),
+                jnp.where(index < nodes + 2 * halo, has_high.astype(F32), 1.0),
+            ),
+        )
+        edge_ok = sender_ok * live_lanes(0, nodes).astype(F32)
+        total = jnp.zeros((wide, nodes), F32)
+        for first in range(0, degree, GROUP_F):
+            slots = range(first, first + GROUP_F)
+            own = [k.early[j] for j in slots] if first < EARLY else own_senders(layer, first)
+            for j, rows in zip(slots, own):
+                chosen = with_halos(layer, j, rows)
+                if layer == 0:
+                    chosen = chosen.astype(BF16)
+                    k.senders[j] = chosen
+                    chosen = dot(k.small[layer, SENDER], chosen)
+                act, slope = gate(chosen + k.pre[j])
+                act = act.astype(BF16)
+                k.act[layer, j] = act
+                k.slope[layer, j] = slope.astype(BF16)
+                second = dot(k.small[layer, SECOND], act)
+                center = second - mean0(second)
+                rate = lax.rsqrt(mean0(center * center) + 1e-05) * edge_ok[j : j + 1]
+                k.rate_e[layer, j : j + 1, :] = rate
+                unit = center * rate
+                k.unit[layer, j] = unit.astype(BF16)
+                total = total + unit
+        k.total[layer] = total
+        k.kept[layer] = jnp.sum(edge_ok, axis=0, keepdims=True)
 
     def nodes_forward(layer, first, last):
-        for lanes in node_lanes(first, last):
+        def act_on(lanes):
             mask = col(layer, CMASK)
             summed = (mask * col(layer, EGAIN)) * k.total[layer, :, lanes] + (
                 mask * col(layer, ESHIFT)
@@ -349,11 +381,13 @@
             else:
                 k.mesh_out[:, lanes] = (k.middle[:, lanes] + change).astype(BF16)
 
+        over_nodes(first, last, act_on)
+
     def into(layer):
         return k.grad_latent if layer == 1 else k.grad_state
 
     def nodes_backward(layer, first, last):
-        for lanes in node_lanes(first, last):
+        def act_on(lanes):
             valid = live_lanes(lanes.start, CHUNK).astype(F32)
             if layer == 1:
                 grad = k.out_grad[:, lanes].astype(F32)
@@ -382,6 +416,8 @@
             k.scaled[:, lanes] = scaled
             k.center[:, lanes] = scaled - mean0(scaled)
 
+        over_nodes(first, last, act_on)
+
     def scatter_slots(lanes, sub, hi, firsts, slots):
         spreads, hots = [], []
         for j, grad in zip(slots, firsts):
@@ -443,22 +479,29 @@
         lax.fori_loop(0, nodes // TILE_B, body, 0)
 
     def edge_weights(layer):
-        grad_two = jnp.zeros((wide, wide), F32)
-        grad_attr = jnp.zeros((wide, wide), F32)
-        grad_both = jnp.zeros((wide, 2 * wide), F32)
-        for j in range(degree):
-            grad_two = grad_two + dot_nt(k.act[layer, j], k.second[j])
+        loops = LOOP_W if layer == 1 else 1
+
+        def body(at, carry):
+            grad_two = jnp.zeros((wide, wide), F32)
+            grad_attr = jnp.zeros((wide, wide), F32)
+            grad_both = jnp.zeros((wide, 2 * wide), F32)
+            for inner in range(degree // loops):
+                j = at * (degree // loops) + inner
+                grad_two = grad_two + dot_nt(k.act[layer, j], k.second[j])
+                if layer == 0:
+                    both = jnp.concatenate([k.senders[j], k.attr[layer, j]], axis=0)
+                    grad_both = grad_both + dot_nt(k.first[j], both)
+                else:
+                    grad_attr = grad_attr + dot_nt(k.first[j], k.attr[layer, j])
+            k.acc_64[layer, 2] += grad_two
             if layer == 0:
-                both = jnp.concatenate([k.senders[j], k.attr[layer, j]], axis=0)
-                grad_both = grad_both + dot_nt(k.first[j], both)
+                k.acc_64[layer, 0] += grad_both[:, :wide]
+                k.acc_64[layer, 1] += grad_both[:, wide:]
             else:
-                grad_attr = grad_attr + dot_nt(k.first[j], k.attr[layer, j])
-        k.acc_64[layer, 2] = grad_two
-        if layer == 0:
-            k.acc_64[layer, 0] = grad_both[:, :wide]
-            k.acc_64[layer, 1] = grad_both[:, wide:]
-        else:
-            k.acc_64[layer, 1] = grad_attr
+                k.acc_64[layer, 1] += grad_attr
+            return carry
+
+        lax.fori_loop(0, loops, body, 0)
 
     def two_terms(values):
         coarse = values.astype(BF16)
@@ -598,6 +641,7 @@
     k.acc_128[...] = jnp.zeros_like(k.acc_128)
     k.scatter[...] = jnp.zeros_like(k.scatter)
     project(0)
+    edges_early(0)
     project_halos(0)
     edges_forward(0)
     fetch["latent"].wait()
@@ -606,6 +650,7 @@
     send_halos(1)
     nodes_forward(0, LISTED, nodes)
     project(1)
+    edges_early(1)
     project_halos(1)
     edges_forward(1)
     fetch["out_grad"].wait()
@@ -767,7 +812,10 @@
         senders=pltpu.VMEM((degree, wide, nodes), BF16),
         first=pltpu.VMEM((degree, wide, nodes), BF16),
         second=pltpu.VMEM((degree, wide, nodes), BF16),
-        table=pltpu.VMEM((parts * wide, high), BF16),
+        table=pltpu.VMEM((nodes // high * wide, high), BF16),
+        far=pltpu.VMEM((wide, 4 * halo), F32),
+        base=pltpu.VMEM((wide, nodes), F32),
+        early=pltpu.VMEM((EARLY, wide, nodes), F32),
         act=pltpu.VMEM((2, degree, wide, nodes), BF16),
         slope=pltpu.VMEM((2, degree, wide, nodes), BF16),
         unit=pltpu.VMEM((2, degree, wide, nodes), BF16),

time: 64.9 us -> 63.1 us (0.972)
  Pallas kernels: 63.2 us -> 61.5 us
    pallas_call x1, Pallas kernels: 60.7 us -> 58.9 us  [shards(): pl.pallas_call(functools.partial(kernel, INPUTS + FIRST_OUTPUTS + tuple(s...]
where the time goes in v1:
time: 63.1 us; the launch traced here: 62.9 us
  Pallas kernels  61.5 us (97%)
  between operations  1.43 us (2%)
    pallas_call x1, Pallas kernels, shards(): pl.pallas_call(functools.partial(kernel, INPUTS + FIRST_OUTPUTS + tuple(s...  58.9 us
    pallas_call x1, Pallas kernels, shards(): pl.pallas_call(functools.partial(finish, FINISH_INPUTS + OUTPUTS), out_sh...  2.56 us

profile of v1, /device:TPU:0, one launch (start us, length us, event | category | flops | bytes accessed | tf_op | source)
XLA Modules:
  0.0 62.9 jit_solution(689047454602208022)
XLA Ops:
  1.3 58.9 %layers.1 = (bf16[64,2048]{1,0:T(8,128)(2,1)}, f32[64,2048]{1,0:T(8,128)}, f32[64,2048]{1,0:T(8,128)}, f32[2,8,32,128]{3,2,1,0:T(8,128)}) custom-call(bf16[64,2048]{1,0:T(8,128)(2,1)} %bitcast.13, bf16[64,2048]{1,0:T(8,128)(2,1)} %bitcast.14, bf16[2,8,64,2048]{3,2,1,0:T(8,128)(2,1)} %bitcast.12, s32[2,8,2048]{2,1,0:T(8,128)} %bitcast.16, s32[4,128]{1,0:T(4,128)} %refs_4_.1, ...), custom_call_target="tpu_custom_call" | custom-call | tf_op jit(solution)/shard_map/layers/pallas_call | solution.py:857
  60.2 2.6 %finish.1 = (bf16[64,2048]{1,0:T(8,128)(2,1)}, f32[64,2048]{1,0:T(8,128)}, f32[64,2048]{1,0:T(8,128)}, f32[2,64,192]{2,1,0:T(8,128)}, f32[2,64]{1,0:T(2,128)}, /...) custom-call(bf16[64,2048]{1,0:T(8,128)(2,1)} %get-tuple-element.30.r, ...), custom_call_target="tpu_custom_call" | custom-call | tf_op jit(solution)/shard_map/finish/pallas_call | solution.py:868

commit v2 on v1

--- a/solution.py
+++ b/solution.py
@@ -555,7 +555,7 @@
         rows = k.share.shape[2]
         for at, block in enumerate(blocks):
             for piece in range(wide // rows):
-                k.share[layer, at * (wide // rows) + piece] = block[
+                k.share[at * (wide // rows) + piece, layer] = block[
                     piece * rows : (piece + 1) * rows, :
                 ].astype(WIRE)
 
@@ -576,55 +576,48 @@
         returned = join([k.backs[layer, way] for way in range(4)])
         into(layer)[:, :LISTED] += dot_nt(returned, k.owner[...])
 
-    def spread_copy(layer, slot, other):
+    def group_copy(source, piece, target, slot, sends, recvs, other, device):
         return pltpu.make_async_remote_copy(
-            src_ref=k.share.at[layer, other],
-            dst_ref=k.spread.at[layer, slot],
-            send_sem=k.rs_send.at[layer, other],
-            recv_sem=k.rs_recv.at[layer, slot],
-            device_id=member_a(other),
+            src_ref=source.at[piece],
+            dst_ref=target.at[slot],
+            send_sem=sends.at[other],
+            recv_sem=recvs.at[slot],
+            device_id=device,
             device_id_type=MESH,
         )
 
-    def swap_copy(layer, slot, other):
-        return pltpu.make_async_remote_copy(
-            src_ref=k.swap.at[layer, at_b],
-            dst_ref=k.swap.at[layer, slot],
-            send_sem=k.sw_send.at[layer, other],
-            recv_sem=k.sw_recv.at[layer, slot],
-            device_id=member_b(other),
-            device_id_type=MESH,
+    def spread_copy(slot, other):
+        return group_copy(
+            k.share, other, k.spread, slot, k.rs_send, k.rs_recv, other, member_a(other)
         )
 
-    def gather_copy(layer, slot, other):
-        return pltpu.make_async_remote_copy(
-            src_ref=k.whole.at[layer, at_a],
-            dst_ref=k.whole.at[layer, slot],
-            send_sem=k.ag_send.at[layer, other],
-            recv_sem=k.ag_recv.at[layer, slot],
-            device_id=member_a(other),
-            device_id_type=MESH,
+    def swap_copy(slot, other):
+        return group_copy(k.swap, at_b, k.swap, slot, k.sw_send, k.sw_recv, other, member_b(other))
+
+    def gather_copy(slot, other):
+        return group_copy(
+            k.whole, at_a, k.whole, slot, k.ag_send, k.ag_recv, other, member_a(other)
         )
 
     def added(blocks):
         return jnp.sum(blocks.astype(F32), axis=0).astype(WIRE)
 
-    def spread_start(layer):
-        over(size_a, at_a, lambda other: spread_copy(layer, at_a, other).start())
-        k.spread[layer, at_a] = k.share[layer, at_a]
-
-    def swap_start(layer):
-        over(size_a, at_a, lambda other: spread_copy(layer, other, other).wait())
-        k.swap[layer, at_b] = added(k.spread[layer])
-        over(size_b, at_b, lambda other: swap_copy(layer, at_b, other).start())
-
-    def gather_start(layer):
-        over(size_b, at_b, lambda other: swap_copy(layer, other, other).wait())
-        k.whole[layer, at_a] = added(k.swap[layer])
-        over(size_a, at_a, lambda other: gather_copy(layer, at_a, other).start())
-
-    def gather_end(layer):
-        over(size_a, at_a, lambda other: gather_copy(layer, other, other).wait())
+    def spread_start():
+        over(size_a, at_a, lambda other: spread_copy(at_a, other).start())
+        k.spread[at_a] = k.share[at_a]
+
+    def swap_start():
+        over(size_a, at_a, lambda other: spread_copy(other, other).wait())
+        k.swap[at_b] = added(k.spread[...])
+        over(size_b, at_b, lambda other: swap_copy(at_b, other).start())
+
+    def gather_start():
+        over(size_b, at_b, lambda other: swap_copy(other, other).wait())
+        k.whole[at_a] = added(k.swap[...])
+        over(size_a, at_a, lambda other: gather_copy(at_a, other).start())
+
+    def gather_end():
+        over(size_a, at_a, lambda other: gather_copy(other, other).wait())
 
     fetch["lists"].wait()
     owners()
@@ -662,7 +655,6 @@
     edge_weights(1)
     sender_weights(1)
     share_weights(1)
-    spread_start(1)
     own_rows(1)
     nodes_backward(0, LISTED, nodes)
     take_back(1)
@@ -671,18 +663,15 @@
     edges_backward(0)
     edge_weights(0)
     share_weights(0)
-    spread_start(0)
-    swap_start(1)
+    spread_start()
     k.scatter[...] = jnp.zeros_like(k.scatter)
-    scatter_pass(0, lambda: swap_start(0))
+    scatter_pass(0, lambda: swap_start())
     give_back(0)
-    gather_start(0)
-    gather_start(1)
+    gather_start()
     own_rows(0)
     take_back(0)
     stores[2].start()
-    gather_end(1)
-    gather_end(0)
+    gather_end()
     stores[3].start()
     for store in stores:
         store.wait()
@@ -699,7 +688,7 @@
         pieces = wide // rows
         blocks = []
         for at in range(4):
-            block = [k.reduced[layer, at * pieces + piece].astype(F32) for piece in range(pieces)]
+            block = [k.reduced[at * pieces + piece, layer].astype(F32) for piece in range(pieces)]
             blocks.append(block[0] if pieces == 1 else jnp.concatenate(block, axis=0))
         k.g_ew1t[layer, :, : 2 * wide] = blocks[0]
         k.g_ew1t[layer, :, 2 * wide :] = blocks[1][:, :wide]
@@ -732,7 +721,7 @@
 FIRST_OUTPUTS = ("mesh_to", "state_to", "latent_to", "reduced")
 FINISH_INPUTS = ("mesh_in", "state_in", "latent_in", "reduced")
 VMEM_BYTES = 60 * 2**20
-WIRE = F32
+WIRE = BF16
 
 
 def shards(bands, lons, *args):
@@ -791,10 +780,10 @@
         backs=pltpu.VMEM((2, 4, wide, halo), BF16),
         sends=pltpu.VMEM((2, 4, wide, halo), BF16),
         gives=pltpu.VMEM((2, 4, wide, halo), BF16),
-        share=pltpu.VMEM((2, size_a, rows, 128), WIRE),
-        spread=pltpu.VMEM((2, size_a, rows, 128), WIRE),
-        swap=pltpu.VMEM((2, size_b, rows, 128), WIRE),
-        whole=pltpu.VMEM((2, size_a, rows, 128), WIRE),
+        share=pltpu.VMEM((size_a, 2, rows, 128), WIRE),
+        spread=pltpu.VMEM((size_a, 2, rows, 128), WIRE),
+        swap=pltpu.VMEM((size_b, 2, rows, 128), WIRE),
+        whole=pltpu.VMEM((size_a, 2, rows, 128), WIRE),
         vrows=pltpu.VMEM((16, wide), F32),
         cols=pltpu.VMEM((wide, 16), F32),
         owner=pltpu.VMEM((LISTED, 4 * halo), BF16),
@@ -838,12 +827,12 @@
         halo_recv=sem((2, 4)),
         back_send=sem((2, 4)),
         back_recv=sem((2, 4)),
-        rs_send=sem((2, size_a)),
-        rs_recv=sem((2, size_a)),
-        sw_send=sem((2, size_b)),
-        sw_recv=sem((2, size_b)),
-        ag_send=sem((2, size_a)),
-        ag_recv=sem((2, size_a)),
+        rs_send=sem((size_a,)),
+        rs_recv=sem((size_a,)),
+        sw_send=sem((size_b,)),
+        sw_recv=sem((size_b,)),
+        ag_send=sem((size_a,)),
+        ag_recv=sem((size_a,)),
     )
     fetched = dict(zip(INPUTS, arrays))
     for name in FETCHED:
@@ -853,7 +842,7 @@
     anywhere = pl.BlockSpec(memory_space=pl.ANY)
     specs = [anywhere] * len(INPUTS)
     specs[INPUTS.index("count")] = pl.BlockSpec(memory_space=pltpu.SMEM)
-    first_outs = outs[:3] + (shape((2, size_a, rows, 128), WIRE),)
+    first_outs = outs[:3] + (shape((size_a, 2, rows, 128), WIRE),)
     mids = pl.pallas_call(
         functools.partial(kernel, INPUTS + FIRST_OUTPUTS + tuple(scratch), bands, lons),
         out_shape=first_outs,

time: 63.1 us -> 60.7 us (0.962)
  Pallas kernels: 61.5 us -> 59 us
    pallas_call x1, Pallas kernels: 58.9 us -> 56.5 us  [shards(): pl.pallas_call(functools.partial(kernel, INPUTS + FIRST_OUTPUTS + tuple(s...]
where the time goes in v2:
time: 60.7 us; the launch traced here: 60.5 us
  Pallas kernels  59 us (97%)
  between operations  1.47 us (2%)
    pallas_call x1, Pallas kernels, shards(): pl.pallas_call(functools.partial(kernel, INPUTS + FIRST_OUTPUTS + tuple(s...  56.5 us
    pallas_call x1, Pallas kernels, shards(): pl.pallas_call(functools.partial(finish, FINISH_INPUTS + OUTPUTS), out_sh...  2.53 us

profile of v2, /device:TPU:0, one launch (start us, length us, event | category | flops | bytes accessed | tf_op | source)
XLA Modules:
  0.0 60.5 jit_solution(18167399063206174709)
XLA Ops:
  1.3 56.5 %layers.1 = (bf16[64,2048]{1,0:T(8,128)(2,1)}, f32[64,2048]{1,0:T(8,128)}, f32[64,2048]{1,0:T(8,128)}, bf16[8,2,32,128]{3,2,1,0:T(8,128)(2,1)}) custom-call(bf16[64,2048]{1,0:T(8,128)(2,1)} %bitcast.13, bf16[64,2048]{1,0:T(8,128)(2,1)} %bitcast.14, bf16[2,8,64,2048]{3,2,1,0:T(8,128)(2,1)} %bitcast.12, s32[2,8,2048]{2,1,0:T(8,128)} %bitcast.16, ...), custom_call_target="tpu_custom_call" | custom-call | tf_op jit(solution)/shard_map/layers/pallas_call | solution.py:846
  57.8 2.5 %finish.1 = (bf16[64,2048]{1,0:T(8,128)(2,1)}, f32[64,2048]{1,0:T(8,128)}, f32[64,2048]{1,0:T(8,128)}, f32[2,64,192]{2,1,0:T(8,128)}, f32[2,64]{1,0:T(2,128)}, /...) custom-call(bf16[64,2048]{1,0:T(8,128)(2,1)} %get-tuple-element.30.r, ...), custom_call_target="tpu_custom_call" | custom-call | tf_op jit(solution)/shard_map/finish/pallas_call | solution.py:857
